TPU v7x, 32 devices: a whole 2x2x4 slice. The times are simulated.
32 devices in a mesh: var: 4 (over y, core), tok: 8 (over z, x).
Axes of the slice: x: 2, y: 2, z: 4, core: 2. Of those that a mesh axis runs over, the one named last changes fastest.
Arguments:
- patches: bfloat16 [72, 4, 1024], P('var', None, 'tok'), may hold values from -6 to 6
- slot_var: int32 [72], replicated, may hold values from -1 to 47, as said below
- patch_weight: bfloat16 [48, 4, 1024], replicated, may hold values from -3 to 3
- var_embed: bfloat16 [48, 1024], replicated, may hold values from -6 to 6
- query: bfloat16 [1024], replicated, may hold values from -16 to 16
- key_weight: bfloat16 [1024, 1024], P('tok'), may hold values from -0.1875 to 0.1875
- value_weight: bfloat16 [1024, 1024], P('tok'), may hold values from -0.1875 to 0.1875
- out_weight: bfloat16 [1024, 1024], P('tok'), may hold values from -0.1875 to 0.1875
- cotangent: bfloat16 [1024, 1024], P(('tok', 'var')), may hold values from -6 to 6
Outputs:
- aggregated: bfloat16 [1024, 1024], P(('tok', 'var'))
- patch_grad: float32 [72, 4096], P('var', 'tok')
Inputs may be any that keep to these rules, and one draw needn't show every extreme that they name: `slot_var`: slot 18 * i + j belongs to index i of var. Every variable id stands in exactly one slot; empty slots hold -1. The live slots of an index come first and hold consecutive ids, rising from index to index. Every index holds at least one and at most 18 live slots, and some index holds exactly 18.
All inputs are finite; a program needn't handle non-finite values.
Results may differ from a plain program's by a relative error of at most 0.011.
Values may be sent and summed in bfloat16 or wider, within the bound.
A program may use at most 128 MiB of HBM per device.

v0:
```python
import functools
import math

import jax
import jax.numpy as jnp
from jax import lax
from jax.experimental import pallas as pl
from jax.experimental.pallas import tpu as pltpu
from jax.sharding import PartitionSpec as P

H = 16
HD = 64

score_cap = 5.0
inv_sqrt_two = 1.0 / math.sqrt(2.0)
inv_sqrt_two_pi = 1.0 / math.sqrt(2.0 * math.pi)

BF = jnp.bfloat16
F32 = jnp.float32
NT = (((1,), (1,)), ((), ()))
TN = (((0,), (0,)), ((), ()))


def main_kernel(
    n_tok,
    n_var,
    pix_ref,
    pw_ref,
    ve_ref,
    wq_ref,
    v_ref,
    o_ref,
    cot_ref,
    sel_ref,
    agg_ref,
    pg_ref,
    e_ref,
    slope_ref,
    g_ref,
    s_ref,
    lhs_ref,
    pe_ref,
    acc_ref,
):
    toks = cot_ref.shape[0]
    width = cot_ref.shape[1]
    lanes = 128
    spans = width // lanes
    tall = H * toks

    def token_rows(ref, t):
        cells = [ref[pl.ds(c * tall + t, H, stride=toks), :] for c in range(spans)]
        return jnp.concatenate(cells, axis=1)

    @pl.loop(0, toks)
    def _(t):
        pix = pix_ref[t]
        pre = ve_ref[...]
        for p in range(4):
            pre = pre + pix[:, p : p + 1] * pw_ref[p]
        cdf = 0.5 * (1.0 + lax.erf(pre * inv_sqrt_two))
        e_ref[t] = (pre * cdf).astype(BF)
        slope_ref[t] = cdf + pre * jnp.exp(-0.5 * pre * pre) * inv_sqrt_two_pi

    gp = lax.dot_general(cot_ref[...], o_ref[...], NT, preferred_element_type=F32)
    low = lax.broadcasted_iota(jnp.int32, (toks, 2 * HD), 1) < HD
    for pair in range(H // 2):
        cols = pl.ds(pair * 2 * HD, 2 * HD)
        part = gp[:, pair * 2 * HD : (pair + 1) * 2 * HD]
        both = jnp.concatenate([jnp.where(low, part, 0.0), jnp.where(low, 0.0, part)], axis=0)
        wide = lax.dot_general(both.astype(BF), v_ref[:, cols], NT, preferred_element_type=F32)
        for c in range(spans):
            rows = pl.ds(c * tall + pair * 2 * toks, 2 * toks)
            g_ref[rows, :] = wide[:, c * lanes : (c + 1) * lanes]

    wq = wq_ref[...]
    wq_hi = wq.astype(BF)
    wq_lo = (wq - wq_hi.astype(F32)).astype(BF)

    @pl.loop(0, toks)
    def _(t):
        g_t = token_rows(g_ref, t).astype(BF)
        rhs = jnp.concatenate([wq_hi, wq_lo, g_t], axis=0)
        s_ref[t] = lax.dot_general(e_ref[t], rhs, NT, preferred_element_type=F32)

    s = s_ref[...]
    raw = (s[:, :, :H] + s[:, :, H : 2 * H]) * (1.0 / math.sqrt(HD))
    grad_attn = s[:, :, 2 * H :]
    squashed = jnp.tanh(raw * (1.0 / score_cap))
    exp_scores = jnp.exp(score_cap * squashed)
    attn = exp_scores / jnp.sum(exp_scores, axis=1, keepdims=True)
    grad_scores = attn * (grad_attn - jnp.sum(attn * grad_attn, axis=1, keepdims=True))
    grad_raw = grad_scores * (1.0 - squashed * squashed) * (1.0 / math.sqrt(HD))
    lhs_ref[...] = jnp.concatenate([attn, grad_raw], axis=2).astype(BF)

    acc_ref[...] = jnp.zeros_like(acc_ref)

    @pl.loop(0, toks)
    def _(t):
        g_t = token_rows(g_ref, t).astype(BF)
        lhs = lhs_ref[t]
        mixed = lax.dot_general(lhs[:, :H], e_ref[t], TN, preferred_element_type=F32)
        for c in range(spans):
            cell = mixed[:, c * lanes : (c + 1) * lanes]
            pe_ref[pl.ds(c * tall + t, H, stride=toks), :] = cell
        rhs = jnp.concatenate([g_t, wq_hi], axis=0)
        grad_pre = jnp.dot(lhs, rhs, preferred_element_type=F32) * slope_ref[t]
        pix = pix_ref[t]
        for p in range(4):
            acc_ref[p] += pix[:, p : p + 1] * grad_pre

    cut = 4 * width // n_tok
    for p in range(4):
        part = acc_ref[p].astype(BF)
        for i in range(n_var):
            rows = jnp.dot(sel_ref[i], part, preferred_element_type=F32).astype(BF)
            for c in range(width // cut):
                k = p * (width // cut) + c
                pg_ref[k * n_var + i] = rows[:, c * cut : (c + 1) * cut]

    pieces = []
    for pair in range(H // 2):
        both = jnp.concatenate(
            [pe_ref[pl.ds(c * tall + pair * 2 * toks, 2 * toks), :] for c in range(spans)],
            axis=1,
        ).astype(BF)
        cols = pl.ds(pair * 2 * HD, 2 * HD)
        two = jnp.dot(both, v_ref[:, cols], preferred_element_type=F32)
        pieces.append(jnp.where(low, two[:toks], two[toks:]))
    pooled = jnp.concatenate(pieces, axis=1).astype(BF)
    agg_ref[...] = jnp.dot(pooled, o_ref[...], preferred_element_type=F32).astype(BF)


def compute(n_tok, n_var, pix, pw, ve, wq, v, o, cot, sel):
    toks, width = cot.shape
    vars_ = ve.shape[0]
    local_slots = sel.shape[1]
    vm = pl.BlockSpec(memory_space=pltpu.VMEM)
    return pl.pallas_call(
        functools.partial(main_kernel, n_tok, n_var),
        out_shape=(
            jax.ShapeDtypeStruct((toks, width), BF),
            jax.ShapeDtypeStruct((n_tok * n_var, local_slots, 4 * width // n_tok), BF),
        ),
        in_specs=[vm] * 8,
        out_specs=(vm, vm),
        scratch_shapes=[
            pltpu.VMEM((toks, vars_, width), BF),
            pltpu.VMEM((toks, vars_, width), F32),
            pltpu.VMEM((width // 128 * H * toks, 128), F32),
            pltpu.VMEM((toks, vars_, 3 * H), F32),
            pltpu.VMEM((toks, vars_, 2 * H), BF),
            pltpu.VMEM((width // 128 * H * toks, 128), F32),
            pltpu.VMEM((4, vars_, width), F32),
        ],
        compiler_params=pltpu.CompilerParams(vmem_limit_bytes=56 * 1024 * 1024),
    )(pix, pw, ve, wq, v, o, cot, sel)


def body(
    n_tok,
    n_var,
    patches,
    slot_var,
    patch_weight,
    var_embed,
    query,
    key_weight,
    value_weight,
    out_weight,
    cotangent,
):
    var_total, _, width = patch_weight.shape
    local_slots = patches.shape[0]
    toks = cotangent.shape[0]
    wq_rows = jnp.einsum(
        "dhj,hj->hd",
        key_weight.reshape(-1, H, HD).astype(F32),
        query.reshape(H, HD).astype(F32),
        precision=lax.Precision.HIGHEST,
    )
    mine = patches.reshape(local_slots, 4, n_var, toks).transpose(2, 0, 1, 3)
    pixels = lax.all_to_all(mine, "var", split_axis=0, concat_axis=0, tiled=True)
    pixels = pixels.reshape(n_var * local_slots, 4 * toks)
    wq = lax.all_gather(wq_rows, "tok", axis=1, tiled=True)
    o = lax.all_gather(out_weight, "tok", axis=0, tiled=True)
    v = lax.all_gather(value_weight, "tok", axis=0, tiled=True)
    picker = slot_var[:, None] == jnp.arange(var_total, dtype=jnp.int32)[None, :]
    picker = picker.astype(BF)
    live = lax.dot_general(picker, pixels, TN, preferred_element_type=F32)
    pix = live.reshape(var_total, 4, toks).transpose(2, 0, 1)
    pw = patch_weight.transpose(1, 0, 2).astype(F32)
    agg, blocks = compute(
        n_tok,
        n_var,
        pix,
        pw,
        var_embed.astype(F32),
        wq,
        v,
        o,
        cotangent,
        picker.reshape(n_var, local_slots, var_total),
    )
    got = lax.all_to_all(blocks, ("tok", "var"), split_axis=0, concat_axis=0, tiled=True)
    return agg, jnp.sum(got.astype(F32), axis=0)


def solution(mesh):
    return jax.shard_map(
        functools.partial(body, mesh.shape["tok"], mesh.shape["var"]),
        mesh=mesh,
        in_specs=(
            P("var", None, "tok"),
            P(),
            P(),
            P(),
            P(),
            P("tok", None),
            P("tok", None),
            P("tok", None),
            P(("tok", "var"), None),
        ),
        out_specs=(P(("tok", "var"), None), P("var", "tok")),
        check_vma=False,
    )
```

profile of v0, /device:TPU:0, one launch (start us, length us, event | category | flops | bytes accessed | tf_op | source)
XLA Modules:
  0.0 174.4 jit_solution(1601077593195300548)
XLA Ops:
  7.2 0.0 copy-start.1
  7.2 0.0 copy-start
  7.2 0.0 all-gather.3.cloned.1.call-start
  7.2 0.7 all-gather.3.cloned.1.call-update
  7.9 0.0 all-gather.5.cloned.1.call-start
  8.0 0.7 all-gather.5.cloned.1.call-update
  8.7 0.8 reshape.27
  9.5 0.7 reshape.36
  10.3 4.2 %all-to-all-start = ((bf16[4,2,1152]{2,1,0:T(2,128)(2,1)}), bf16[4,2,1152]{2,1,0:T(2,128)(2,1)S(1)}, u32[]{:S(2)}, u32[]{:S(2)}) async-start(bf16[4,2,1152]{2,1,0:T(2,128)(2,1)} %reshape.36), calls=%async_computation | async-start | bytes 36864 | tf_op jit(solution)/shard_map/all_to_all | solution.py:183
  14.5 0.7 eq.25
  15.2 0.8 reshape.35
  16.0 1.1 copy.18
  17.1 0.7 fusion.sel_ref
  17.8 0.2 fusion.5
  18.0 2.0 %convert_bitcast_fusion.pw_ref = f32[4,48,1024]{2,1,0:T(8,128)} fusion(bf16[48,4,1024]{2,1,0:T(4,128)(2,1)} %param.11), kind=kLoop, calls=%fused_computation.1 | loop fusion | flops 196608 | bytes 1179648 | tf_op jit(solution)/shard_map/convert_element_type | solution.py:192
  20.0 33.4 %all_gather.9.wq_ref = f32[16,1024]{1,0:T(8,128)} all-gather(f32[16,128]{1,0:T(8,128)S(1)} %bitcast.22), channel_id=1, replica_groups=mesh['var'=4,'tok'=8] {'tok'}, dimensions={1}, use_global_device_ids=true | all-gather | bytes 73728 | tf_op jit(solution)/shard_map/all_gather | solution.py:185
  53.4 0.0 copy-done
  53.4 0.7 convert_element_type.19.ve_ref
  54.1 0.0 all-to-all-done
  54.1 0.1 reshape.37
  54.2 0.1 reshape.28
  54.3 0.1 copy.15
  54.5 0.0 copy-done.1
  54.5 0.1 fusion.2
  54.6 1.3 copy.16
  55.9 6.4 %all-gather.3.cloned.1.call-done.v_ref = bf16[1024,1024]{1,0:T(8,128)(2,1)} async-done(((bf16[128,1024]{1,0:T(8,128)(2,1)}), bf16[1024,1024]{1,0:T(8,128)(2,1)}) %all-gather.3.cloned.1.call-update) | async-done | bytes 2097168 | tf_op jit(solution)/shard_map/all_gather | solution.py:187
  62.2 50.5 %all-gather.5.cloned.1.call-done.o_ref = bf16[1024,1024]{1,0:T(8,128)(2,1)} async-done(((bf16[128,1024]{1,0:T(8,128)(2,1)}), bf16[1024,1024]{1,0:T(8,128)(2,1)}) %all-gather.5.cloned.1.call-update) | async-done | bytes 2097168 | tf_op jit(solution)/shard_map/all_gather | solution.py:186
  112.7 30.4 %shard_map.104 = (bf16[32,1024]{1,0:T(8,128)(2,1)}, bf16[32,18,512]{2,1,0:T(8,128)(2,1)}) custom-call(f32[32,48,4]{2,1,0:T(8,128)} %bitcast.17, f32[4,48,1024]{2,1,0:T(8,128)} %convert_bitcast_fusion.pw_ref, f32[48,1024]{1,0:T(8,128)} %convert_element_type.19.ve_ref, f32[16,1024]{1,0:T(8,128)} %all_gather.9.wq_ref, ...), custom_call_target="tpu_custom_call" | custom-call | tf_op jit(solution)/shard_map/pallas_call | solution.py:139
  143.1 23.7 %all_to_all.10 = bf16[32,18,512]{2,1,0:T(8,128)(2,1)S(1)} all-to-all(bf16[32,18,512]{2,1,0:T(8,128)(2,1)} %get-tuple-element.5), channel_id=1, replica_groups=mesh['var'=4,'tok'=8] {'tok','var'}, dimensions={0} | all-to-all | bytes 1179648 | tf_op jit(solution)/shard_map/all_to_all | solution.py:205
  166.8 0.8 convert_reduce_fusion
  (1 shorter events, 0.0 us)
Async XLA Ops:
  7.2 47.3 %copy-start.1 = (s32[72]{0:T(128)S(1)}, s32[72]{0:T(128)}, u32[]{:S(2)}) copy-start(s32[72]{0:T(128)} %param.10) | copy-start | bytes 868
  7.2 46.2 %copy-start = (bf16[48,1024]{1,0:T(8,128)(2,1)S(1)}, bf16[48,1024]{1,0:T(8,128)(2,1)}, u32[]{:S(2)}) copy-start(bf16[48,1024]{1,0:T(8,128)(2,1)} %param.12) | copy-start | bytes 294916
  7.2 55.0 %all-gather.3.cloned.1.call-start = ((), (), s32[]{:S(2)}) async-start(), calls=%async_computation.2 | async-start | bytes 2359296 | tf_op jit(solution)/shard_map/all_gather | solution.py:187
  7.9 104.8 %all-gather.5.cloned.1.call-start = ((), (), s32[]{:S(2)}) async-start(), calls=%async_computation.3 | async-start | bytes 2359296 | tf_op jit(solution)/shard_map/all_gather | solution.py:186
  10.3 43.9 %all-to-all-start = ((bf16[4,2,1152]{2,1,0:T(2,128)(2,1)}), bf16[4,2,1152]{2,1,0:T(2,128)(2,1)S(1)}, u32[]{:S(2)}, u32[]{:S(2)}) async-start(bf16[4,2,1152]{2,1,0:T(2,128)(2,1)} %reshape.36), calls=%async_computation | async-start | bytes 36864 | tf_op jit(solution)/shard_map/all_to_all | solution.py:183
Sparse Core Ops, SparseCore 0:
  10.1 52.0 all-gather.2
  64.3 48.3 all-gather.4
where the time goes:
time: 175 us; the launch traced here: 174 us
  waiting for transfers between devices  58.2 us (33%)
  blocking collectives  57.1 us (33%)
  Pallas kernels  30.4 us (17%)
  between operations  14.1 us (8%)
  local copies, waits for them, and re-layouts  5.78 us (3%)
  starting transfers between devices  4.31 us (2%)
  other arithmetic  4.18 us (2%)
    all_gather x1, waiting for transfers between devices, body(): o = lax.all_gather(out_weight, 'tok', axis=0, tiled=True)  50.5 us
    all_gather x1, blocking collectives, body(): wq = lax.all_gather(wq_rows, 'tok', axis=1, tiled=True)  33.4 us
    pallas_call x1, Pallas kernels, compute(): pl.pallas_call(functools.partial(main_kernel, n_tok, n_var), out_shape=(j...  30.4 us
    all_to_all x1, blocking collectives, body(): lax.all_to_all(blocks, ('tok', 'var'), split_axis=0, concat_axis=0, tiled...  23.7 us
    all_gather x1, waiting for transfers between devices, body(): v = lax.all_gather(value_weight, 'tok', axis=0, tiled=True)  6.36 us
    all_to_all x1, starting transfers between devices, body(): lax.all_to_all(mine, 'var', split_axis=0, concat_axis=0, tiled=True)  4.24 us
  transfers between devices with their start and end apart: 3, of which 2 were waited for; matrix products, arithmetic and copies ran while one was open for 5% of the time, Pallas kernels for 0%

commit v1 on v0

v1 whole, which is shorter than its diff:
```python
import functools
import math

import jax
import jax.numpy as jnp
from jax import lax
from jax.experimental import pallas as pl
from jax.experimental.pallas import tpu as pltpu
from jax.sharding import PartitionSpec as P

H = 16
HD = 64

score_cap = 5.0
inv_sqrt_two = 1.0 / math.sqrt(2.0)
inv_sqrt_two_pi = 1.0 / math.sqrt(2.0 * math.pi)

BF = jnp.bfloat16
F32 = jnp.float32
NT = (((1,), (1,)), ((), ()))
TN = (((0,), (0,)), ((), ()))


def all_kernel(
    n_tok,
    n_var,
    pat_ref,
    wqs_ref,
    wsh_ref,
    pw_ref,
    ve_ref,
    cot_ref,
    sel_ref,
    spread_ref,
    agg_ref,
    sum_ref,
    pixels_ref,
    wqa_ref,
    w_ref,
    pix_ref,
    e_ref,
    slope_ref,
    g_ref,
    s_ref,
    lhs_ref,
    pe_ref,
    acc_ref,
    out_ref,
    in_ref,
    pat_send,
    pat_recv,
    wq_send,
    wq_recv,
    tok_send,
    tok_recv,
    row_send,
    row_recv,
    sib_send,
    sib_recv,
    sum_send,
    sum_recv,
):
    toks, width = cot_ref.shape
    rows = wsh_ref.shape[0]
    lanes = 128
    spans = width // lanes
    tall = H * toks
    total = n_tok * n_var
    wide = 2 * width // n_var
    pairs = n_var // 2
    block = 256
    me_t = lax.axis_index("tok")
    me_v = lax.axis_index("var")
    me = me_t * n_var + me_v
    sibling = me_v + 1 - 2 * lax.rem(me_v, 2)

    def remote(src, dst, send, recv, **place):
        return pltpu.make_async_remote_copy(
            src_ref=src,
            dst_ref=dst,
            send_sem=send,
            recv_sem=recv,
            device_id=place,
            device_id_type=pl.DeviceIdType.MESH,
        )

    def peer(n):
        at = lax.rem(me + n, total)
        return {"tok": at // n_var, "var": lax.rem(at, n_var)}

    barrier = pltpu.get_barrier_semaphore()

    @pl.loop(1, total)
    def _(n):
        pl.semaphore_signal(
            barrier, inc=1, device_id=peer(n), device_id_type=pl.DeviceIdType.MESH
        )

    pl.semaphore_wait(barrier, total - 1)

    pat_copies = []
    for n in range(1, n_var):
        to = lax.rem(me_v + n, n_var)
        copy = remote(
            pat_ref.at[to], pixels_ref.at[me_v], pat_send.at[n], pat_recv.at[n], var=to
        )
        copy.start()
        pat_copies.append(copy)
    wq_copies = []
    tok_copies = []
    for n in range(1, n_tok):
        to = lax.rem(me_t + n, n_tok)
        spot = (
            pl.ds(pl.multiple_of(me_t * rows, rows), rows),
            pl.ds(pl.multiple_of(me_v * wide, wide), wide),
        )
        copy = remote(wsh_ref.at[:, spot[1]], w_ref.at[spot], tok_send.at[n], tok_recv.at[n], tok=to)
        copy.start()
        tok_copies.append(copy)
        copy = remote(wqs_ref, wqa_ref.at[me_t], wq_send.at[n], wq_recv.at[n], tok=to)
        copy.start()
        wq_copies.append(copy)

    pixels_ref[me_v] = pat_ref[me_v]
    wqa_ref[me_t] = wqs_ref[...]
    w_ref[pl.ds(pl.multiple_of(me_t * rows, rows), rows), :] = wsh_ref[...]
    acc_ref[...] = jnp.zeros_like(acc_ref)

    row_copies = []
    sib_copies = []

    def to_sibling(n, m, spot):
        at = (n - 1) * pairs + m
        copy = remote(w_ref.at[spot], w_ref.at[spot], sib_send.at[at], sib_recv.at[at], var=sibling)
        copy.start()
        sib_copies.append(copy)

    def place_of(n, m):
        source = lax.rem(me_t + n_tok - n, n_tok)
        owner = lax.rem(me_v + n_var - 2 * m, n_var)
        return (
            pl.ds(pl.multiple_of(source * rows, rows), rows),
            pl.ds(pl.multiple_of(owner * wide, wide), wide),
        )

    def pass_first(n):
        tok_copies[n - 1].wait_recv()
        spot = place_of(n, 0)
        for m in range(1, pairs):
            at = (n - 1) * (pairs - 1) + m - 1
            to = lax.rem(me_v + 2 * m, n_var)
            copy = remote(w_ref.at[spot], w_ref.at[spot], row_send.at[at], row_recv.at[at], var=to)
            copy.start()
            row_copies.append(copy)
        to_sibling(n, 0, spot)

    def pass_second(n):
        for m in range(1, pairs):
            row_copies[(n - 1) * (pairs - 1) + m - 1].wait_recv()
            to_sibling(n, m, place_of(n, m))

    for copy in pat_copies:
        copy.wait_recv()
    live = lax.dot_general(sel_ref[0], pixels_ref[0], TN, preferred_element_type=F32)
    for i in range(1, n_var):
        live += lax.dot_general(sel_ref[i], pixels_ref[i], TN, preferred_element_type=F32)
    lane_at = lax.broadcasted_iota(jnp.int32, live.shape, 1)

    def embed(first, count):
        @pl.loop(first, first + count)
        def _(t):
            cols = []
            for p in range(4):
                col = jnp.sum(
                    jnp.where(lane_at == p * toks + t, live, 0.0), axis=1, keepdims=True
                )
                pix_ref[t, :, p : p + 1] = col
                cols.append(col)
            for c in range(0, width, block):
                span = slice(c, c + block)
                pre = ve_ref[:, span]
                for p in range(4):
                    pre = pre + cols[p] * pw_ref[p, :, span]
                cdf = 0.5 * (1.0 + lax.erf(pre * inv_sqrt_two))
                e_ref[t, :, span] = (pre * cdf).astype(BF)
                slope_ref[t, :, span] = cdf + pre * jnp.exp(-0.5 * pre * pre) * inv_sqrt_two_pi

    steps = 8
    first_done, second_done = 1, 1
    for c in range(steps):
        embed(c * (toks // steps), toks // steps)
        upto = 1 + (c + 1) * (n_tok - 1) // steps
        while second_done < first_done:
            pass_second(second_done)
            second_done += 1
        while first_done < upto:
            pass_first(first_done)
            first_done += 1
    while second_done < first_done:
        pass_second(second_done)
        second_done += 1

    for copy in wq_copies:
        copy.wait_recv()
    for copy in sib_copies:
        copy.wait_recv()

    gp = lax.dot_general(cot_ref[...], w_ref[:, width:], NT, preferred_element_type=F32)
    low = lax.broadcasted_iota(jnp.int32, (toks, 2 * HD), 1) < HD
    for pair in range(H // 2):
        part = gp[:, pair * 2 * HD : (pair + 1) * 2 * HD]
        both = jnp.concatenate([jnp.where(low, part, 0.0), jnp.where(low, 0.0, part)], axis=0)
        carried = lax.dot_general(
            both.astype(BF),
            w_ref[:, pair * 2 * HD : (pair + 1) * 2 * HD],
            NT,
            preferred_element_type=F32,
        )
        for c in range(spans):
            g_ref[pl.ds(c * tall + pair * 2 * toks, 2 * toks), :] = carried[
                :, c * lanes : (c + 1) * lanes
            ]

    def token_rows(t):
        cells = [g_ref[pl.ds(c * tall + t, H, stride=toks), :] for c in range(spans)]
        return jnp.concatenate(cells, axis=1).astype(BF)

    wq = jnp.concatenate([wqa_ref[k] for k in range(n_tok)], axis=1)
    wq_hi = wq.astype(BF)
    wq_lo = (wq - wq_hi.astype(F32)).astype(BF)
    group = 4

    @pl.loop(0, toks // group)
    def _(step):
        for u in range(group):
            t = step * group + u
            rhs = jnp.concatenate([wq_hi, wq_lo, token_rows(t)], axis=0)
            s_ref[t] = lax.dot_general(e_ref[t], rhs, NT, preferred_element_type=F32)

    s = s_ref[...]
    raw = (s[:, :, :H] + s[:, :, H : 2 * H]) * (1.0 / math.sqrt(HD))
    grad_attn = s[:, :, 2 * H :]
    squashed = jnp.tanh(raw * (1.0 / score_cap))
    exp_scores = jnp.exp(score_cap * squashed)
    attn = exp_scores / jnp.sum(exp_scores, axis=1, keepdims=True)
    grad_scores = attn * (grad_attn - jnp.sum(attn * grad_attn, axis=1, keepdims=True))
    grad_raw = grad_scores * (1.0 - squashed * squashed) * (1.0 / math.sqrt(HD))
    lhs_ref[...] = jnp.concatenate([attn, grad_raw], axis=2).astype(BF)

    @pl.loop(0, toks // group)
    def _(step):
        cols, left, right = [], [], []
        for u in range(group):
            t = step * group + u
            lhs = lhs_ref[t]
            mixed = lax.dot_general(lhs[:, :H], e_ref[t], TN, preferred_element_type=F32)
            for c in range(spans):
                cell = mixed[:, c * lanes : (c + 1) * lanes]
                pe_ref[pl.ds(c * tall + t, H, stride=toks), :] = cell
            left.append(lhs)
            right.append(jnp.concatenate([token_rows(t), wq_hi], axis=0))
            pix = pix_ref[t]
            cols.append([pix[:, p : p + 1] for p in range(4)])
        for c in range(0, width, block):
            span = slice(c, c + block)
            grads = [
                jnp.dot(left[u], right[u][:, span], preferred_element_type=F32)
                * slope_ref[step * group + u, :, span]
                for u in range(group)
            ]
            for p in range(4):
                more = cols[0][p] * grads[0]
                for u in range(1, group):
                    more = more + cols[u][p] * grads[u]
                acc_ref[p, :, span] += more

    cut = 4 * width // n_tok
    chunks = cut // lanes
    tall_out = in_ref.shape[1]
    for k in range(n_tok):
        p, start = k * cut // width, k * cut % width
        stacked = jnp.concatenate(
            [
                acc_ref[p, :, start + c * lanes : start + (c + 1) * lanes].astype(BF)
                for c in range(chunks)
            ],
            axis=0,
        )
        placed = jnp.dot(spread_ref[...], stacked, preferred_element_type=F32).astype(BF)
        for i in range(n_var):
            out_ref[k * n_var + i] = placed[i * tall_out : (i + 1) * tall_out]

    @pl.loop(1, total)
    def _(n):
        to = peer(n)
        at = to["tok"] * n_var + to["var"]
        remote(out_ref.at[at], in_ref.at[n], sum_send.at[n], sum_recv.at[n], **to).start()

    pieces = []
    for pair in range(H // 2):
        both = jnp.concatenate(
            [pe_ref[pl.ds(c * tall + pair * 2 * toks, 2 * toks), :] for c in range(spans)],
            axis=1,
        ).astype(BF)
        two = jnp.dot(
            both, w_ref[:, pair * 2 * HD : (pair + 1) * 2 * HD], preferred_element_type=F32
        )
        pieces.append(jnp.where(low, two[:toks], two[toks:]))
    pooled = jnp.concatenate(pieces, axis=1).astype(BF)
    agg_ref[...] = jnp.dot(pooled, w_ref[:, width:], preferred_element_type=F32).astype(BF)

    sum_ref[...] = out_ref[me].astype(F32)

    @pl.loop(1, total)
    def _(n):
        to = peer(n)
        at = to["tok"] * n_var + to["var"]
        copy = remote(out_ref.at[at], in_ref.at[n], sum_send.at[n], sum_recv.at[n], **to)
        copy.wait()
        sum_ref[...] += in_ref[n].astype(F32)

    for copy in pat_copies + wq_copies + tok_copies + row_copies + sib_copies:
        copy.wait_send()


def compute(n_tok, n_var, pat, wqs, wsh, pw, ve, cot, sel, spread):
    toks, width = cot.shape
    vars_ = ve.shape[0]
    rows = wsh.shape[0]
    pairs = n_var // 2
    total = n_tok * n_var
    tall_out = spread.shape[0] // n_var
    vm = pl.BlockSpec(memory_space=pltpu.VMEM)
    dma = pltpu.SemaphoreType.DMA
    return pl.pallas_call(
        functools.partial(all_kernel, n_tok, n_var),
        out_shape=(
            jax.ShapeDtypeStruct((toks, width), BF),
            jax.ShapeDtypeStruct((tall_out, 128), F32),
        ),
        in_specs=[vm] * 8,
        out_specs=(vm, vm),
        scratch_shapes=[
            pltpu.VMEM(pat.shape, BF),
            pltpu.VMEM((n_tok,) + wqs.shape, F32),
            pltpu.VMEM((width, 2 * width), BF),
            pltpu.VMEM((toks, vars_, 4), F32),
            pltpu.VMEM((toks, vars_, width), BF),
            pltpu.VMEM((toks, vars_, width), F32),
            pltpu.VMEM((width // 128 * H * toks, 128), F32),
            pltpu.VMEM((toks, vars_, 3 * H), F32),
            pltpu.VMEM((toks, vars_, 2 * H), BF),
            pltpu.VMEM((width // 128 * H * toks, 128), F32),
            pltpu.VMEM((4, vars_, width), F32),
            pltpu.VMEM((total, tall_out, 128), BF),
            pltpu.VMEM((total, tall_out, 128), BF),
            dma((n_var,)),
            dma((n_var,)),
            dma((n_tok,)),
            dma((n_tok,)),
            dma((n_tok,)),
            dma((n_tok,)),
            dma((n_tok * pairs,)),
            dma((n_tok * pairs,)),
            dma((n_tok * pairs,)),
            dma((n_tok * pairs,)),
            dma((total,)),
            dma((total,)),
        ],
        compiler_params=pltpu.CompilerParams(
            vmem_limit_bytes=56 * 1024 * 1024, collective_id=0, has_side_effects=True
        ),
    )(pat, wqs, wsh, pw, ve, cot, sel, spread)


def body(
    n_tok,
    n_var,
    patches,
    slot_var,
    patch_weight,
    var_embed,
    query,
    key_weight,
    value_weight,
    out_weight,
    cotangent,
):
    var_total, _, width = patch_weight.shape
    local_slots = patches.shape[0]
    toks = cotangent.shape[0]
    wq_rows = jnp.einsum(
        "dhj,hj->hd",
        key_weight.reshape(-1, H, HD).astype(F32),
        query.reshape(H, HD).astype(F32),
        precision=lax.Precision.HIGHEST,
    )
    pad = -local_slots % 16
    mine = patches.reshape(local_slots, 4, n_var, toks).transpose(2, 0, 1, 3)
    mine = mine.reshape(n_var, local_slots, 4 * toks)
    mine = jnp.pad(mine, ((0, 0), (0, pad), (0, 0)))
    picker = slot_var[:, None] == jnp.arange(var_total, dtype=jnp.int32)[None, :]
    picker = picker.astype(BF).reshape(n_var, local_slots, var_total)
    chunks = 4 * width // n_tok // 128
    spread = jnp.einsum("isv,cb->icsbv", picker, jnp.eye(chunks, dtype=BF))
    spread = spread.reshape(n_var, chunks * local_slots, chunks * var_total)
    spread = jnp.pad(spread, ((0, 0), (0, -(chunks * local_slots) % 16), (0, 0)))
    agg, sums = compute(
        n_tok,
        n_var,
        mine,
        wq_rows,
        jnp.concatenate([value_weight, out_weight], axis=1),
        patch_weight.transpose(1, 0, 2).astype(F32),
        var_embed.astype(F32),
        cotangent,
        jnp.pad(picker, ((0, 0), (0, pad), (0, 0))),
        spread.reshape(-1, chunks * var_total),
    )
    sums = sums[: chunks * local_slots].reshape(chunks, local_slots, 128)
    return agg, sums.transpose(1, 0, 2).reshape(local_slots, chunks * 128)


def solution(mesh):
    return jax.shard_map(
        functools.partial(body, mesh.shape["tok"], mesh.shape["var"]),
        mesh=mesh,
        in_specs=(
            P("var", None, "tok"),
            P(),
            P(),
            P(),
            P(),
            P("tok", None),
            P("tok", None),
            P("tok", None),
            P(("tok", "var"), None),
        ),
        out_specs=(P(("tok", "var"), None), P("var", "tok")),
        check_vma=False,
    )
```

time: 175 us -> 90 us (0.51)
  the two profiles are of different devices: /device:TPU:0 before, /device:TPU:19 now
where the time goes in v1:
time: 90 us; the launch traced here: 89.6 us
  Pallas kernels  78.7 us (87%)
  local copies, waits for them, and re-layouts  6.46 us (7%)
  other arithmetic  2.82 us (3%)
    pallas_call x1, Pallas kernels, compute(): pl.pallas_call(functools.partial(all_kernel, n_tok, n_var), out_shape=(ja...  78.7 us
    unnamed x20, local copies, waits for them, and re-layouts  2.5 us

profile of v1, /device:TPU:19, one launch (start us, length us, event | category | flops | bytes accessed | tf_op | source)
XLA Modules:
  0.0 89.6 jit_solution(11573225038383298917)
XLA Ops:
  0.6 0.0 copy-start.7
  0.7 0.7 eq.20
  1.4 0.0 copy-done.7
  1.4 0.1 reshape.56
  1.5 0.1 fusion
  1.6 0.0 copy-start.6
  1.6 0.6 pad.13.sel_ref
  2.2 0.1 copy-done.6
  2.3 0.1 reshape.45
  2.4 0.0 copy-start.4
  2.4 0.0 copy-start.1
  2.4 0.1 reshape.46
  2.6 0.6 pad.12.pat_ref
  3.2 0.1 copy-done.4
  3.3 0.7 convert_element_type.23.ve_ref
  4.0 0.0 copy-done.1
  4.0 0.2 copy.20
  4.2 0.8 fusion.2
  4.9 0.2 multiply_bitcast_fusion
  5.1 0.0 copy-start.3
  5.1 0.2 reshape.49
  5.3 0.0 copy-start.2
  5.3 0.7 pad.14
  6.0 0.0 copy-done.3
  6.1 0.3 copy-done.2
  6.4 0.0 copy-start
  6.4 0.8 pad_maximum_fusion.wsh_ref
  7.2 0.3 copy-done
  7.5 1.0 %convert_bitcast_fusion.pw_ref = f32[4,48,1024]{2,1,0:T(8,128)} fusion(bf16[48,4,1024]{2,1,0:T(4,128)(2,1)S(1)} %copy-done), kind=kLoop, calls=%fused_computation | loop fusion | flops 196608 | bytes 1179648 | tf_op jit(solution)/shard_map/convert_element_type | solution.py:414
  8.5 78.7 %shard_map.104 = (bf16[32,1024]{1,0:T(8,128)(2,1)}, f32[80,128]{1,0:T(8,128)}) custom-call(bf16[4,32,128]{2,1,0:T(8,128)(2,1)} %pad.12.pat_ref, f32[16,128]{1,0:T(8,128)} %bitcast.25, bf16[128,2048]{1,0:T(8,128)(2,1)} %pad_maximum_fusion.wsh_ref, f32[4,48,1024]{2,1,0:T(8,128)} %convert_bitcast_fusion.pw_ref, f32[48,1024]{1,0:T(8,128)} %convert_element_type.23.ve_ref, ...), custom_call_target="tpu_custom_call" | custom-call | tf_op jit(solution)/shard_map/pallas_call | solution.py:335
  87.3 0.8 slice.3
  88.1 0.0 copy-start.5
  88.1 0.6 copy.25
  88.7 0.2 copy-done.5
  89.0 0.6 copy.30
  (6 shorter events, 0.1 us)
Async XLA Ops:
  0.6 0.8 copy-start.7
  1.6 0.7 copy-start.6
  2.4 0.9 copy-start.4
  2.4 1.5 %copy-start.1 = (bf16[128,1024]{1,0:T(8,128)(2,1)S(1)}, bf16[128,1024]{1,0:T(8,128)(2,1)}, u32[]{:S(2)}) copy-start(bf16[128,1024]{1,0:T(8,128)(2,1)} %param.14) | copy-start | bytes 786436
  5.1 1.0 %copy-start.3 = (bf16[128,1024]{1,0:T(8,128)(2,1)S(1)}, bf16[128,1024]{1,0:T(8,128)(2,1)}, u32[]{:S(2)}) copy-start(bf16[128,1024]{1,0:T(8,128)(2,1)} %param.15) | copy-start | bytes 786436
  5.3 1.0 %copy-start.2 = (bf16[128,1024]{1,0:T(8,128)(2,1)S(1)}, bf16[128,1024]{1,0:T(8,128)(2,1)}, u32[]{:S(2)}) copy-start(bf16[128,1024]{1,0:T(8,128)(2,1)} %param.16) | copy-start | bytes 786436
  6.4 1.2 %copy-start = (bf16[48,4,1024]{2,1,0:T(4,128)(2,1)S(1)}, bf16[48,4,1024]{2,1,0:T(4,128)(2,1)}, u32[]{:S(2)}) copy-start(bf16[48,4,1024]{2,1,0:T(4,128)(2,1)} %param.11) | copy-start | bytes 1179652
  88.1 0.9 copy-start.5

commit v2 on v1

v2 whole, which is shorter than its diff:
```python
import functools
import math

import jax
import jax.numpy as jnp
from jax import lax
from jax.experimental import pallas as pl
from jax.experimental.pallas import tpu as pltpu
from jax.sharding import PartitionSpec as P

H = 16
HD = 64

score_cap = 5.0
inv_sqrt_two = 1.0 / math.sqrt(2.0)
inv_sqrt_two_pi = 1.0 / math.sqrt(2.0 * math.pi)

BF = jnp.bfloat16
F32 = jnp.float32
NT = (((1,), (1,)), ((), ()))
TN = (((0,), (0,)), ((), ()))


def all_kernel(
    n_tok,
    n_var,
    pat_ref,
    slot_ref,
    query_ref,
    kw_ref,
    vw_ref,
    ow_ref,
    pw_ref,
    ve_ref,
    cot_ref,
    agg_ref,
    sum_ref,
    total_ref,
    pixels_ref,
    wqs_ref,
    wqa_ref,
    w_ref,
    pix_ref,
    e_ref,
    slope_ref,
    g_ref,
    attn_ref,
    slope_s_ref,
    s_ref,
    lhs_ref,
    pe_ref,
    acc_ref,
    out_ref,
    in_ref,
    pat_send,
    pat_recv,
    wq_send,
    wq_recv,
    tok_send,
    tok_recv,
    row_send,
    row_recv,
    sib_send,
    sib_recv,
    sum_send,
    sum_recv,
):
    toks, width = cot_ref.shape
    rows = vw_ref.shape[0]
    vars_ = ve_ref.shape[0]
    slots = slot_ref.shape[1]
    local_slots = slots // n_var
    lanes = 128
    spans = width // lanes
    tall = H * toks
    total = n_tok * n_var
    wide = 2 * width // n_var
    pairs = n_var // 2
    block = 256
    me_t = lax.axis_index("tok")
    me_v = lax.axis_index("var")
    me = me_t * n_var + me_v
    sibling = me_v + 1 - 2 * lax.rem(me_v, 2)

    def remote(src, dst, send, recv, **place):
        return pltpu.make_async_remote_copy(
            src_ref=src,
            dst_ref=dst,
            send_sem=send,
            recv_sem=recv,
            device_id=place,
            device_id_type=pl.DeviceIdType.MESH,
        )

    def peer(n):
        at = lax.rem(me + n, total)
        return {"tok": at // n_var, "var": lax.rem(at, n_var)}

    barrier = pltpu.get_barrier_semaphore()

    @pl.loop(1, total)
    def _(n):
        pl.semaphore_signal(
            barrier, inc=1, device_id=peer(n), device_id_type=pl.DeviceIdType.MESH
        )

    pl.semaphore_wait(barrier, total - 1)

    pat_copies = []
    for n in range(1, n_var):
        to = lax.rem(me_v + n, n_var)
        copy = remote(
            pat_ref.at[to], pixels_ref.at[me_v], pat_send.at[n], pat_recv.at[n], var=to
        )
        copy.start()
        pat_copies.append(copy)
    own_rows = pl.ds(pl.multiple_of(me_t * rows, rows), rows)
    w_ref[own_rows, :width] = vw_ref[...]
    w_ref[own_rows, width:] = ow_ref[...]
    spot = (own_rows, pl.ds(pl.multiple_of(me_v * wide, wide), wide))
    tok_copies = []
    for n in range(1, n_tok):
        to = lax.rem(me_t + n, n_tok)
        copy = remote(w_ref.at[spot], w_ref.at[spot], tok_send.at[n], tok_recv.at[n], tok=to)
        copy.start()
        tok_copies.append(copy)

    head_of = lax.broadcasted_iota(jnp.int32, (H, width), 1) // HD
    heads = (head_of == lax.broadcasted_iota(jnp.int32, (H, width), 0)).astype(F32).astype(BF)
    seen = kw_ref[...].astype(F32) * query_ref[...].astype(F32)
    seen_hi = seen.astype(BF)
    seen_lo = (seen - seen_hi.astype(F32)).astype(BF)
    wqs_ref[...] = lax.dot_general(
        heads, seen_hi, NT, preferred_element_type=F32
    ) + lax.dot_general(heads, seen_lo, NT, preferred_element_type=F32)
    wq_copies = []
    for n in range(1, n_tok):
        to = lax.rem(me_t + n, n_tok)
        copy = remote(wqs_ref, wqa_ref.at[me_t], wq_send.at[n], wq_recv.at[n], tok=to)
        copy.start()
        wq_copies.append(copy)

    pixels_ref[me_v] = pat_ref[me_v]
    wqa_ref[me_t] = wqs_ref[...]
    acc_ref[...] = jnp.zeros_like(acc_ref)

    picker = (
        lax.broadcasted_iota(jnp.int32, (vars_, slots), 0) == slot_ref[...]
    ).astype(F32).astype(BF)

    def slot_rows(count, tall_one, copies):
        at = lax.broadcasted_iota(jnp.int32, (count, slots), 0)
        slot = lax.broadcasted_iota(jnp.int32, (count, slots), 1)
        within = at % tall_one
        live_row = within < copies * local_slots
        match = slot == (at // tall_one) * local_slots + within % local_slots
        return (live_row & match).astype(F32).astype(BF), within // local_slots

    row_copies = []
    sib_copies = []

    def to_sibling(n, m, spot):
        at = (n - 1) * pairs + m
        copy = remote(w_ref.at[spot], w_ref.at[spot], sib_send.at[at], sib_recv.at[at], var=sibling)
        copy.start()
        sib_copies.append(copy)

    def place_of(n, m):
        source = lax.rem(me_t + n_tok - n, n_tok)
        owner = lax.rem(me_v + n_var - 2 * m, n_var)
        return (
            pl.ds(pl.multiple_of(source * rows, rows), rows),
            pl.ds(pl.multiple_of(owner * wide, wide), wide),
        )

    def pass_first(n):
        tok_copies[n - 1].wait_recv()
        spot = place_of(n, 0)
        for m in range(1, pairs):
            at = (n - 1) * (pairs - 1) + m - 1
            to = lax.rem(me_v + 2 * m, n_var)
            copy = remote(w_ref.at[spot], w_ref.at[spot], row_send.at[at], row_recv.at[at], var=to)
            copy.start()
            row_copies.append(copy)
        to_sibling(n, 0, spot)

    def pass_second(n):
        for m in range(1, pairs):
            row_copies[(n - 1) * (pairs - 1) + m - 1].wait_recv()
            to_sibling(n, m, place_of(n, m))

    for copy in pat_copies:
        copy.wait_recv()
    held = pat_ref.shape[1]
    unpad, _ = slot_rows(n_var * held, held, 1)
    chooser = lax.dot_general(picker, unpad, NT, preferred_element_type=F32).astype(BF)
    live = jnp.dot(chooser, pixels_ref[...].reshape(n_var * held, -1), preferred_element_type=F32)
    lane_at = lax.broadcasted_iota(jnp.int32, live.shape, 1)

    def embed(first, count):
        @pl.loop(first, first + count)
        def _(t):
            cols = []
            for p in range(4):
                col = jnp.sum(
                    jnp.where(lane_at == p * toks + t, live, 0.0), axis=1, keepdims=True
                )
                pix_ref[t, :, p : p + 1] = col
                cols.append(col)
            for c in range(0, width, block):
                span = slice(c, c + block)
                pre = ve_ref[:, span].astype(F32)
                for p in range(4):
                    pre = pre + cols[p] * pw_ref[p, :, span]
                cdf = 0.5 * (1.0 + lax.erf(pre * inv_sqrt_two))
                e_ref[t, :, span] = (pre * cdf).astype(BF)
                slope_ref[t, :, span] = cdf + pre * jnp.exp(-0.5 * pre * pre) * inv_sqrt_two_pi

    def attend(first, count):
        flat = e_ref[first : first + count].reshape(count * vars_, width)
        both = lax.dot_general(flat, wq_both, NT, preferred_element_type=F32)
        both = both.reshape(count, vars_, 2 * H)
        raw = (both[:, :, :H] + both[:, :, H:]) * (1.0 / math.sqrt(HD))
        squashed = jnp.tanh(raw * (1.0 / score_cap))
        exp_scores = jnp.exp(score_cap * squashed)
        attn = exp_scores / jnp.sum(exp_scores, axis=1, keepdims=True)
        attn_ref[first : first + count] = attn
        slope_s_ref[first : first + count] = (
            attn * (1.0 - squashed * squashed) * (1.0 / math.sqrt(HD))
        )
        for u in range(count):
            mixed = lax.dot_general(
                attn[u].astype(BF), e_ref[first + u], TN, preferred_element_type=F32
            )
            for c in range(spans):
                cell = mixed[:, c * lanes : (c + 1) * lanes]
                pe_ref[pl.ds(c * tall + first + u, H, stride=toks), :] = cell

    steps = 8
    first_done, second_done = 1, 1
    for c in range(steps):
        each = toks // steps
        embed(c * each, each)
        if c == 0:
            for copy in wq_copies:
                copy.wait_recv()
            wq = jnp.concatenate([wqa_ref[k] for k in range(n_tok)], axis=1)
            wq_hi = wq.astype(BF)
            wq_lo = (wq - wq_hi.astype(F32)).astype(BF)
            wq_both = jnp.concatenate([wq_hi, wq_lo], axis=0)
        attend(c * each, each)
        upto = 1 + (c + 1) * (n_tok - 1) // steps
        while second_done < first_done:
            pass_second(second_done)
            second_done += 1
        while first_done < upto:
            pass_first(first_done)
            first_done += 1
    while second_done < first_done:
        pass_second(second_done)
        second_done += 1

    for copy in sib_copies:
        copy.wait_recv()

    gp = lax.dot_general(cot_ref[...], w_ref[:, width:], NT, preferred_element_type=F32)
    low = lax.broadcasted_iota(jnp.int32, (toks, 2 * HD), 1) < HD
    for pair in range(H // 2):
        part = gp[:, pair * 2 * HD : (pair + 1) * 2 * HD]
        both = jnp.concatenate([jnp.where(low, part, 0.0), jnp.where(low, 0.0, part)], axis=0)
        carried = lax.dot_general(
            both.astype(BF),
            w_ref[:, pair * 2 * HD : (pair + 1) * 2 * HD],
            NT,
            preferred_element_type=F32,
        )
        for c in range(spans):
            g_ref[pl.ds(c * tall + pair * 2 * toks, 2 * toks), :] = carried[
                :, c * lanes : (c + 1) * lanes
            ]

    def token_rows(t, first, count):
        cells = [g_ref[pl.ds(c * tall + t, H, stride=toks), :] for c in range(first, first + count)]
        return jnp.concatenate(cells, axis=1).astype(BF)

    group = 4

    @pl.loop(0, toks // group)
    def _(step):
        for u in range(group):
            t = step * group + u
            rhs = token_rows(t, 0, spans)
            s_ref[t] = lax.dot_general(e_ref[t], rhs, NT, preferred_element_type=F32)

    attn = attn_ref[...]
    grad_attn = s_ref[...]
    grad_raw = slope_s_ref[...] * (grad_attn - jnp.sum(attn * grad_attn, axis=1, keepdims=True))
    lhs_ref[...] = jnp.concatenate([attn, grad_raw], axis=2).astype(BF)

    cut = 4 * width // n_tok
    chunks = cut // lanes
    tall_out = in_ref.shape[1]
    place, chunk_of = slot_rows(n_var * tall_out, tall_out, chunks)
    placed = lax.dot_general(place, picker, NT, preferred_element_type=F32).astype(BF)
    chunk_of = chunk_of[:, :1]
    spread = jnp.concatenate(
        [jnp.where(chunk_of == c, placed, jnp.zeros_like(placed)) for c in range(chunks)], axis=1
    )
    half = width // 2
    per = half // cut
    count = 4 * per

    for h in range(2):

        @pl.loop(0, toks // group)
        def _(step):
            cols, left, right = [], [], []
            for u in range(group):
                t = step * group + u
                left.append(lhs_ref[t])
                mine = token_rows(t, h * spans // 2, spans // 2)
                right.append(
                    jnp.concatenate([mine, wq_hi[:, h * half : (h + 1) * half]], axis=0)
                )
                pix = pix_ref[t]
                cols.append([pix[:, p : p + 1] for p in range(4)])
            for c in range(0, half, block):
                span = slice(h * half + c, h * half + c + block)
                grads = [
                    jnp.dot(left[u], right[u][:, c : c + block], preferred_element_type=F32)
                    * slope_ref[step * group + u, :, span]
                    for u in range(group)
                ]
                for p in range(4):
                    more = cols[0][p] * grads[0]
                    for u in range(1, group):
                        more = more + cols[u][p] * grads[u]
                    acc_ref[p, :, span] += more

        for a in range(count):
            p, start = a // per, h * half + a % per * cut
            k = p * 2 * per + h * per + a % per
            stacked = jnp.concatenate(
                [
                    acc_ref[p, :, start + c * lanes : start + (c + 1) * lanes].astype(BF)
                    for c in range(chunks)
                ],
                axis=0,
            )
            out = jnp.dot(spread, stacked, preferred_element_type=F32).astype(BF)
            for i in range(n_var):
                out_ref[k * n_var + i] = out[i * tall_out : (i + 1) * tall_out]

        @pl.loop(0, count * n_var)
        def _(n):
            a = lax.rem(me_t // 2 + n // n_var, count)
            k = a // per * 2 * per + h * per + lax.rem(a, per)
            i = lax.rem(me_v + lax.rem(n, n_var), n_var)
            at = k * n_var + i

            @pl.when(at != me)
            def _():
                remote(
                    out_ref.at[at], in_ref.at[me], sum_send.at[at], sum_recv.at[me], tok=k, var=i
                ).start()

    pieces = []
    for pair in range(H // 2):
        both = jnp.concatenate(
            [pe_ref[pl.ds(c * tall + pair * 2 * toks, 2 * toks), :] for c in range(spans)],
            axis=1,
        ).astype(BF)
        two = jnp.dot(
            both, w_ref[:, pair * 2 * HD : (pair + 1) * 2 * HD], preferred_element_type=F32
        )
        pieces.append(jnp.where(low, two[:toks], two[toks:]))
    pooled = jnp.concatenate(pieces, axis=1).astype(BF)
    agg_ref[...] = jnp.dot(pooled, w_ref[:, width:], preferred_element_type=F32).astype(BF)

    total_ref[...] = out_ref[me].astype(F32)

    @pl.loop(1, total)
    def _(n):
        to = peer(n)
        at = to["tok"] * n_var + to["var"]
        copy = remote(out_ref.at[at], in_ref.at[at], sum_send.at[at], sum_recv.at[at], **to)
        copy.wait()
        total_ref[...] += in_ref[at].astype(F32)

    for c in range(chunks):
        sum_ref[:, c * lanes : (c + 1) * lanes] = total_ref[
            c * local_slots : (c + 1) * local_slots, :
        ]

    for copy in pat_copies + wq_copies + tok_copies + row_copies + sib_copies:
        copy.wait_send()


def compute(n_tok, n_var, pat, slot, query, kw, vw, ow, pw, ve, cot):
    toks, width = cot.shape
    vars_ = ve.shape[0]
    rows = vw.shape[0]
    local_slots = slot.shape[1] // n_var
    pairs = n_var // 2
    total = n_tok * n_var
    chunks = 4 * width // n_tok // 128
    tall_out = -(-chunks * local_slots // 16) * 16
    vm = pl.BlockSpec(memory_space=pltpu.VMEM)
    dma = pltpu.SemaphoreType.DMA
    return pl.pallas_call(
        functools.partial(all_kernel, n_tok, n_var),
        out_shape=(
            jax.ShapeDtypeStruct((toks, width), BF),
            jax.ShapeDtypeStruct((local_slots, chunks * 128), F32),
        ),
        in_specs=[vm] * 9,
        out_specs=(vm, vm),
        scratch_shapes=[
            pltpu.VMEM((tall_out, 128), F32),
            pltpu.VMEM(pat.shape, BF),
            pltpu.VMEM((H, rows), F32),
            pltpu.VMEM((n_tok, H, rows), F32),
            pltpu.VMEM((width, 2 * width), BF),
            pltpu.VMEM((toks, vars_, 4), F32),
            pltpu.VMEM((toks, vars_, width), BF),
            pltpu.VMEM((toks, vars_, width), F32),
            pltpu.VMEM((width // 128 * H * toks, 128), F32),
            pltpu.VMEM((toks, vars_, H), F32),
            pltpu.VMEM((toks, vars_, H), F32),
            pltpu.VMEM((toks, vars_, H), F32),
            pltpu.VMEM((toks, vars_, 2 * H), BF),
            pltpu.VMEM((width // 128 * H * toks, 128), F32),
            pltpu.VMEM((4, vars_, width), F32),
            pltpu.VMEM((total, tall_out, 128), BF),
            pltpu.VMEM((total, tall_out, 128), BF),
            dma((n_var,)),
            dma((n_var,)),
            dma((n_tok,)),
            dma((n_tok,)),
            dma((n_tok,)),
            dma((n_tok,)),
            dma((n_tok * pairs,)),
            dma((n_tok * pairs,)),
            dma((n_tok * pairs,)),
            dma((n_tok * pairs,)),
            dma((total,)),
            dma((total,)),
        ],
        compiler_params=pltpu.CompilerParams(
            vmem_limit_bytes=56 * 1024 * 1024, collective_id=0, has_side_effects=True
        ),
    )(pat, slot, query, kw, vw, ow, pw, ve, cot)


def body(
    n_tok,
    n_var,
    patches,
    slot_var,
    patch_weight,
    var_embed,
    query,
    key_weight,
    value_weight,
    out_weight,
    cotangent,
):
    local_slots = patches.shape[0]
    toks = cotangent.shape[0]
    mine = patches.reshape(local_slots, 4, n_var, toks).transpose(2, 0, 1, 3)
    mine = mine.reshape(n_var, local_slots, 4 * toks)
    mine = jnp.pad(mine, ((0, 0), (0, -local_slots % 16), (0, 0)))
    return compute(
        n_tok,
        n_var,
        mine,
        slot_var.reshape(1, -1),
        query.reshape(1, -1),
        key_weight,
        value_weight,
        out_weight,
        patch_weight.transpose(1, 0, 2).astype(F32),
        var_embed,
        cotangent,
    )


def solution(mesh):
    return jax.shard_map(
        functools.partial(body, mesh.shape["tok"], mesh.shape["var"]),
        mesh=mesh,
        in_specs=(
            P("var", None, "tok"),
            P(),
            P(),
            P(),
            P(),
            P("tok", None),
            P("tok", None),
            P("tok", None),
            P(("tok", "var"), None),
        ),
        out_specs=(P(("tok", "var"), None), P("var", "tok")),
        check_vma=False,
    )
```

time: 90 us -> 99.1 us (1.10)
  the two profiles are of different devices: /device:TPU:19 before, /device:TPU:27 now
where the time goes in v2:
time: 99.1 us; the launch traced here: 98.3 us
  Pallas kernels  91.6 us (92%)
  local copies, waits for them, and re-layouts  5.01 us (5%)
  other arithmetic  1.02 us (1%)
    pallas_call x1, Pallas kernels, compute(): pl.pallas_call(functools.partial(all_kernel, n_tok, n_var), out_shape=(ja...  91.6 us
    unnamed x6, local copies, waits for them, and re-layouts  2.11 us

profile of v2, /device:TPU:27, one launch (start us, length us, event | category | flops | bytes accessed | tf_op | source)
XLA Modules:
  0.0 98.3 jit_solution(12508424145137872136)
XLA Ops:
  0.6 0.0 copy-start
  0.6 1.3 %reshape.19.query_ref = bf16[1,1024]{1,0:T(2,128)(2,1)} reshape(bf16[1024]{0:T(1024)(128)(2,1)} %param.13) | data formatting | bytes 4096 | tf_op jit(solution)/shard_map/reshape | solution.py:478
  2.0 0.8 reshape.16
  2.8 0.1 reshape.17
  2.9 0.6 pad.4.pat_ref
  3.6 0.0 copy-done
  3.6 1.0 %convert_bitcast_fusion.pw_ref = f32[4,48,1024]{2,1,0:T(8,128)} fusion(bf16[48,4,1024]{2,1,0:T(4,128)(2,1)S(1)} %copy-done), kind=kLoop, calls=%fused_computation | loop fusion | flops 196608 | bytes 1179648 | tf_op jit(solution)/shard_map/convert_element_type | solution.py:482
  4.6 91.6 %shard_map.104 = (bf16[32,1024]{1,0:T(8,128)(2,1)}, f32[18,512]{1,0:T(8,128)}) custom-call(bf16[4,32,128]{2,1,0:T(8,128)(2,1)} %pad.4.pat_ref, s32[1,72]{1,0:T(1,128)} %bitcast.9, bf16[1,1024]{1,0:T(2,128)(2,1)} %reshape.19.query_ref, bf16[128,1024]{1,0:T(8,128)(2,1)} %kw_ref.1, bf16[128,1024]{1,0:T(8,128)(2,1)} %vw_ref.1, bf16[128,1024]{1,0:T(8,128)(2,1)} %ow_ref.1, ...), custom_call_target="tpu_custom_call" | custom-call | tf_op jit(solution)/shard_map/pallas_call | solution.py:410
  96.2 0.0 copy-start.1
  96.2 1.5 %copy.21 = bf16[32,1024]{1,0:T(8,128)(2,1)} copy(bf16[32,1024]{1,0:T(8,128)(2,1)} %get-tuple-element.4) | data formatting | bytes 131072
  97.7 0.0 copy-done.1
  97.7 0.6 copy.22
  (2 shorter events, 0.0 us)
Async XLA Ops:
  0.6 2.9 %copy-start = (bf16[48,4,1024]{2,1,0:T(4,128)(2,1)S(1)}, bf16[48,4,1024]{2,1,0:T(4,128)(2,1)}, u32[]{:S(2)}) copy-start(bf16[48,4,1024]{2,1,0:T(4,128)(2,1)} %param.11) | copy-start | bytes 1179652
  96.2 1.5 %copy-start.1 = (f32[18,512]{1,0:T(8,128)S(1)}, f32[18,512]{1,0:T(8,128)}, u32[]{:S(2)}) copy-start(f32[18,512]{1,0:T(8,128)} %get-tuple-element.5) | copy-start | bytes 110596

commit v3 on v2

--- a/solution.py
+++ b/solution.py
@@ -46,7 +46,8 @@
     g_ref,
     attn_ref,
     slope_s_ref,
-    s_ref,
+    wqb_ref,
+    pooled_ref,
     lhs_ref,
     pe_ref,
     acc_ref,
@@ -118,12 +119,22 @@
     w_ref[own_rows, :width] = vw_ref[...]
     w_ref[own_rows, width:] = ow_ref[...]
     spot = (own_rows, pl.ds(pl.multiple_of(me_v * wide, wide), wide))
-    tok_copies = []
-    for n in range(1, n_tok):
+
+    def offset(j):
+        odd = lax.rem(j, 2)
+        return odd * ((j + 1) // 2) + (1 - odd) * (n_tok - j // 2)
+
+    def tok_copy(n):
         to = lax.rem(me_t + n, n_tok)
-        copy = remote(w_ref.at[spot], w_ref.at[spot], tok_send.at[n], tok_recv.at[n], tok=to)
-        copy.start()
-        tok_copies.append(copy)
+        return remote(w_ref.at[spot], w_ref.at[spot], tok_send.at[n], tok_recv.at[n], tok=to)
+
+    def wq_copy(n):
+        to = lax.rem(me_t + n, n_tok)
+        return remote(wqs_ref, wqa_ref.at[me_t], wq_send.at[n], wq_recv.at[n], tok=to)
+
+    @pl.loop(1, n_tok)
+    def _(j):
+        tok_copy(offset(j)).start()
 
     head_of = lax.broadcasted_iota(jnp.int32, (H, width), 1) // HD
     heads = (head_of == lax.broadcasted_iota(jnp.int32, (H, width), 0)).astype(F32).astype(BF)
@@ -133,12 +144,10 @@
     wqs_ref[...] = lax.dot_general(
         heads, seen_hi, NT, preferred_element_type=F32
     ) + lax.dot_general(heads, seen_lo, NT, preferred_element_type=F32)
-    wq_copies = []
-    for n in range(1, n_tok):
-        to = lax.rem(me_t + n, n_tok)
-        copy = remote(wqs_ref, wqa_ref.at[me_t], wq_send.at[n], wq_recv.at[n], tok=to)
-        copy.start()
-        wq_copies.append(copy)
+
+    @pl.loop(1, n_tok)
+    def _(j):
+        wq_copy(offset(j)).start()
 
     pixels_ref[me_v] = pat_ref[me_v]
     wqa_ref[me_t] = wqs_ref[...]
@@ -156,15 +165,6 @@
         match = slot == (at // tall_one) * local_slots + within % local_slots
         return (live_row & match).astype(F32).astype(BF), within // local_slots
 
-    row_copies = []
-    sib_copies = []
-
-    def to_sibling(n, m, spot):
-        at = (n - 1) * pairs + m
-        copy = remote(w_ref.at[spot], w_ref.at[spot], sib_send.at[at], sib_recv.at[at], var=sibling)
-        copy.start()
-        sib_copies.append(copy)
-
     def place_of(n, m):
         source = lax.rem(me_t + n_tok - n, n_tok)
         owner = lax.rem(me_v + n_var - 2 * m, n_var)
@@ -173,21 +173,33 @@
             pl.ds(pl.multiple_of(owner * wide, wide), wide),
         )
 
-    def pass_first(n):
-        tok_copies[n - 1].wait_recv()
-        spot = place_of(n, 0)
-        for m in range(1, pairs):
-            at = (n - 1) * (pairs - 1) + m - 1
-            to = lax.rem(me_v + 2 * m, n_var)
-            copy = remote(w_ref.at[spot], w_ref.at[spot], row_send.at[at], row_recv.at[at], var=to)
-            copy.start()
-            row_copies.append(copy)
-        to_sibling(n, 0, spot)
-
-    def pass_second(n):
-        for m in range(1, pairs):
-            row_copies[(n - 1) * (pairs - 1) + m - 1].wait_recv()
-            to_sibling(n, m, place_of(n, m))
+    def sib_copy(n, m):
+        where = place_of(n, m)
+        at = (n - 1) * pairs + m
+        return remote(w_ref.at[where], w_ref.at[where], sib_send.at[at], sib_recv.at[at], var=sibling)
+
+    def row_copy(n, m):
+        where = place_of(n, 0)
+        at = (n - 1) * (pairs - 1) + m - 1
+        to = lax.rem(me_v + 2 * m, n_var)
+        return remote(w_ref.at[where], w_ref.at[where], row_send.at[at], row_recv.at[at], var=to)
+
+    def pass_first(first, last):
+        @pl.loop(first, last)
+        def _(j):
+            n = offset(j)
+            tok_copy(n).wait_recv()
+            for m in range(1, pairs):
+                row_copy(n, m).start()
+            sib_copy(n, 0).start()
+
+    def pass_second(first, last):
+        @pl.loop(first, last)
+        def _(j):
+            n = offset(j)
+            for m in range(1, pairs):
+                row_copy(n, m).wait_recv()
+                sib_copy(n, m).start()
 
     for copy in pat_copies:
         copy.wait_recv()
@@ -197,38 +209,59 @@
     live = jnp.dot(chooser, pixels_ref[...].reshape(n_var * held, -1), preferred_element_type=F32)
     lane_at = lax.broadcasted_iota(jnp.int32, live.shape, 1)
 
-    def embed(first, count):
-        @pl.loop(first, first + count)
-        def _(t):
-            cols = []
+    def passed(t):
+        return lax.max(t + 1, 0) * (n_tok - 1) // toks
+
+    lag = 4
+
+    @pl.loop(0, toks)
+    def _(t):
+        cols = []
+        for p in range(4):
+            col = jnp.sum(jnp.where(lane_at == p * toks + t, live, 0.0), axis=1, keepdims=True)
+            pix_ref[t, :, p : p + 1] = col
+            cols.append(col)
+
+        @pl.loop(0, width // block)
+        def _(c):
+            span = pl.ds(pl.multiple_of(c * block, block), block)
+            pre = ve_ref[:, span].astype(F32)
             for p in range(4):
-                col = jnp.sum(
-                    jnp.where(lane_at == p * toks + t, live, 0.0), axis=1, keepdims=True
-                )
-                pix_ref[t, :, p : p + 1] = col
-                cols.append(col)
-            for c in range(0, width, block):
-                span = slice(c, c + block)
-                pre = ve_ref[:, span].astype(F32)
-                for p in range(4):
-                    pre = pre + cols[p] * pw_ref[p, :, span]
-                cdf = 0.5 * (1.0 + lax.erf(pre * inv_sqrt_two))
-                e_ref[t, :, span] = (pre * cdf).astype(BF)
-                slope_ref[t, :, span] = cdf + pre * jnp.exp(-0.5 * pre * pre) * inv_sqrt_two_pi
-
-    def attend(first, count):
-        flat = e_ref[first : first + count].reshape(count * vars_, width)
-        both = lax.dot_general(flat, wq_both, NT, preferred_element_type=F32)
-        both = both.reshape(count, vars_, 2 * H)
+                pre = pre + cols[p] * pw_ref[p, :, span]
+            cdf = 0.5 * (1.0 + lax.erf(pre * inv_sqrt_two))
+            e_ref[t, :, span] = (pre * cdf).astype(BF)
+            slope_ref[t, :, span] = cdf + pre * jnp.exp(-0.5 * pre * pre) * inv_sqrt_two_pi
+
+        pass_second(passed(t - lag - 1) + 1, passed(t - lag) + 1)
+        pass_first(passed(t - 1) + 1, passed(t) + 1)
+
+    @pl.loop(1, n_tok)
+    def _(n):
+        wq_copy(n).wait_recv()
+
+    wq = jnp.concatenate([wqa_ref[k] for k in range(n_tok)], axis=1)
+    wq_hi = wq.astype(BF)
+    wqb_ref[:H] = wq_hi
+    wqb_ref[H:] = (wq - wq_hi.astype(F32)).astype(BF)
+    pass_second((toks - lag) * (n_tok - 1) // toks + 1, n_tok)
+
+    group = 4
+
+    @pl.loop(0, toks // group)
+    def _(step):
+        first = step * group
+        flat = e_ref[pl.ds(first, group)].reshape(group * vars_, width)
+        both = lax.dot_general(flat, wqb_ref[...], NT, preferred_element_type=F32)
+        both = both.reshape(group, vars_, 2 * H)
         raw = (both[:, :, :H] + both[:, :, H:]) * (1.0 / math.sqrt(HD))
         squashed = jnp.tanh(raw * (1.0 / score_cap))
         exp_scores = jnp.exp(score_cap * squashed)
         attn = exp_scores / jnp.sum(exp_scores, axis=1, keepdims=True)
-        attn_ref[first : first + count] = attn
-        slope_s_ref[first : first + count] = (
+        attn_ref[pl.ds(first, group)] = attn
+        slope_s_ref[pl.ds(first, group)] = (
             attn * (1.0 - squashed * squashed) * (1.0 / math.sqrt(HD))
         )
-        for u in range(count):
+        for u in range(group):
             mixed = lax.dot_general(
                 attn[u].astype(BF), e_ref[first + u], TN, preferred_element_type=F32
             )
@@ -236,66 +269,39 @@
                 cell = mixed[:, c * lanes : (c + 1) * lanes]
                 pe_ref[pl.ds(c * tall + first + u, H, stride=toks), :] = cell
 
-    steps = 8
-    first_done, second_done = 1, 1
-    for c in range(steps):
-        each = toks // steps
-        embed(c * each, each)
-        if c == 0:
-            for copy in wq_copies:
-                copy.wait_recv()
-            wq = jnp.concatenate([wqa_ref[k] for k in range(n_tok)], axis=1)
-            wq_hi = wq.astype(BF)
-            wq_lo = (wq - wq_hi.astype(F32)).astype(BF)
-            wq_both = jnp.concatenate([wq_hi, wq_lo], axis=0)
-        attend(c * each, each)
-        upto = 1 + (c + 1) * (n_tok - 1) // steps
-        while second_done < first_done:
-            pass_second(second_done)
-            second_done += 1
-        while first_done < upto:
-            pass_first(first_done)
-            first_done += 1
-    while second_done < first_done:
-        pass_second(second_done)
-        second_done += 1
-
-    for copy in sib_copies:
-        copy.wait_recv()
-
-    gp = lax.dot_general(cot_ref[...], w_ref[:, width:], NT, preferred_element_type=F32)
+    @pl.loop(1, n_tok)
+    def _(n):
+        for m in range(pairs):
+            sib_copy(n, m).wait_recv()
+
     low = lax.broadcasted_iota(jnp.int32, (toks, 2 * HD), 1) < HD
-    for pair in range(H // 2):
-        part = gp[:, pair * 2 * HD : (pair + 1) * 2 * HD]
+
+    @pl.loop(0, H // 2)
+    def _(pair):
+        cols = pl.ds(pl.multiple_of(pair * 2 * HD, 2 * HD), 2 * HD)
+        part = lax.dot_general(cot_ref[...], w_ref[cols, width:], NT, preferred_element_type=F32)
         both = jnp.concatenate([jnp.where(low, part, 0.0), jnp.where(low, 0.0, part)], axis=0)
-        carried = lax.dot_general(
-            both.astype(BF),
-            w_ref[:, pair * 2 * HD : (pair + 1) * 2 * HD],
-            NT,
-            preferred_element_type=F32,
-        )
+        carried = lax.dot_general(both.astype(BF), w_ref[:, cols], NT, preferred_element_type=F32)
         for c in range(spans):
-            g_ref[pl.ds(c * tall + pair * 2 * toks, 2 * toks), :] = carried[
-                :, c * lanes : (c + 1) * lanes
-            ]
+            at = pl.multiple_of(c * tall + pair * 2 * toks, 2 * toks)
+            g_ref[pl.ds(at, 2 * toks), :] = carried[:, c * lanes : (c + 1) * lanes]
 
     def token_rows(t, first, count):
         cells = [g_ref[pl.ds(c * tall + t, H, stride=toks), :] for c in range(first, first + count)]
         return jnp.concatenate(cells, axis=1).astype(BF)
-
-    group = 4
 
     @pl.loop(0, toks // group)
     def _(step):
         for u in range(group):
             t = step * group + u
-            rhs = token_rows(t, 0, spans)
-            s_ref[t] = lax.dot_general(e_ref[t], rhs, NT, preferred_element_type=F32)
-
-    attn = attn_ref[...]
-    grad_attn = s_ref[...]
-    grad_raw = slope_s_ref[...] * (grad_attn - jnp.sum(attn * grad_attn, axis=1, keepdims=True))
-    lhs_ref[...] = jnp.concatenate([attn, grad_raw], axis=2).astype(BF)
+            grad_attn = lax.dot_general(
+                e_ref[t], token_rows(t, 0, spans), NT, preferred_element_type=F32
+            )
+            attn = attn_ref[t]
+            mean = jnp.sum(attn * grad_attn, axis=0, keepdims=True)
+            lhs_ref[t] = jnp.concatenate(
+                [attn, slope_s_ref[t] * (grad_attn - mean)], axis=1
+            ).astype(BF)
 
     cut = 4 * width // n_tok
     chunks = cut // lanes
@@ -320,7 +326,7 @@
                 left.append(lhs_ref[t])
                 mine = token_rows(t, h * spans // 2, spans // 2)
                 right.append(
-                    jnp.concatenate([mine, wq_hi[:, h * half : (h + 1) * half]], axis=0)
+                    jnp.concatenate([mine, wqb_ref[:H, h * half : (h + 1) * half]], axis=0)
                 )
                 pix = pix_ref[t]
                 cols.append([pix[:, p : p + 1] for p in range(4)])
@@ -364,18 +370,25 @@
                     out_ref.at[at], in_ref.at[me], sum_send.at[at], sum_recv.at[me], tok=k, var=i
                 ).start()
 
-    pieces = []
-    for pair in range(H // 2):
+    @pl.loop(0, H // 2)
+    def _(pair):
+        cols = pl.ds(pl.multiple_of(pair * 2 * HD, 2 * HD), 2 * HD)
         both = jnp.concatenate(
-            [pe_ref[pl.ds(c * tall + pair * 2 * toks, 2 * toks), :] for c in range(spans)],
+            [
+                pe_ref[pl.ds(pl.multiple_of(c * tall + pair * 2 * toks, 2 * toks), 2 * toks), :]
+                for c in range(spans)
+            ],
             axis=1,
         ).astype(BF)
-        two = jnp.dot(
-            both, w_ref[:, pair * 2 * HD : (pair + 1) * 2 * HD], preferred_element_type=F32
-        )
-        pieces.append(jnp.where(low, two[:toks], two[toks:]))
-    pooled = jnp.concatenate(pieces, axis=1).astype(BF)
-    agg_ref[...] = jnp.dot(pooled, w_ref[:, width:], preferred_element_type=F32).astype(BF)
+        two = jnp.dot(both, w_ref[:, cols], preferred_element_type=F32)
+        pooled_ref[:, cols] = jnp.where(low, two[:toks], two[toks:]).astype(BF)
+
+    @pl.loop(0, width // block)
+    def _(c):
+        at = pl.multiple_of(c * block, block)
+        agg_ref[:, pl.ds(at, block)] = jnp.dot(
+            pooled_ref[...], w_ref[:, pl.ds(width + at, block)], preferred_element_type=F32
+        ).astype(BF)
 
     total_ref[...] = out_ref[me].astype(F32)
 
@@ -392,8 +405,17 @@
             c * local_slots : (c + 1) * local_slots, :
         ]
 
-    for copy in pat_copies + wq_copies + tok_copies + row_copies + sib_copies:
+    for copy in pat_copies:
         copy.wait_send()
+
+    @pl.loop(1, n_tok)
+    def _(n):
+        wq_copy(n).wait_send()
+        tok_copy(n).wait_send()
+        for m in range(1, pairs):
+            row_copy(n, m).wait_send()
+        for m in range(pairs):
+            sib_copy(n, m).wait_send()
 
 
 def compute(n_tok, n_var, pat, slot, query, kw, vw, ow, pw, ve, cot):
@@ -427,7 +449,8 @@
             pltpu.VMEM((width // 128 * H * toks, 128), F32),
             pltpu.VMEM((toks, vars_, H), F32),
             pltpu.VMEM((toks, vars_, H), F32),
-            pltpu.VMEM((toks, vars_, H), F32),
+            pltpu.VMEM((2 * H, width), BF),
+            pltpu.VMEM((toks, width), BF),
             pltpu.VMEM((toks, vars_, 2 * H), BF),
             pltpu.VMEM((width // 128 * H * toks, 128), F32),
             pltpu.VMEM((4, vars_, width), F32),

time: 99.1 us -> 82.4 us (0.83)
  Pallas kernels: 91.6 us -> 75.4 us
    pallas_call x1, Pallas kernels: 91.6 us -> 75.4 us  [compute(): pl.pallas_call(functools.partial(all_kernel, n_tok, n_var), out_shape=(ja...]
where the time goes in v3:
time: 82.4 us; the launch traced here: 82.2 us
  Pallas kernels  75.4 us (92%)
  local copies, waits for them, and re-layouts  5.01 us (6%)
  other arithmetic  1.02 us (1%)
    pallas_call x1, Pallas kernels, compute(): pl.pallas_call(functools.partial(all_kernel, n_tok, n_var), out_shape=(ja...  75.4 us
    unnamed x6, local copies, waits for them, and re-layouts  2.11 us

profile of v3, /device:TPU:27, one launch (start us, length us, event | category | flops | bytes accessed | tf_op | source)
XLA Modules:
  0.0 82.2 jit_solution(1421033397803298210)
XLA Ops:
  0.6 0.0 copy-start
  0.6 1.3 %reshape.19.query_ref = bf16[1,1024]{1,0:T(2,128)(2,1)} reshape(bf16[1024]{0:T(1024)(128)(2,1)} %param.13) | data formatting | bytes 4096 | tf_op jit(solution)/shard_map/reshape | solution.py:501
  2.0 0.8 reshape.16
  2.8 0.1 reshape.17
  2.9 0.6 pad.4.pat_ref
  3.6 0.0 copy-done
  3.6 1.0 %convert_bitcast_fusion.pw_ref = f32[4,48,1024]{2,1,0:T(8,128)} fusion(bf16[48,4,1024]{2,1,0:T(4,128)(2,1)S(1)} %copy-done), kind=kLoop, calls=%fused_computation | loop fusion | flops 196608 | bytes 1179648 | tf_op jit(solution)/shard_map/convert_element_type | solution.py:505
  4.6 75.4 %shard_map.104 = (bf16[32,1024]{1,0:T(8,128)(2,1)}, f32[18,512]{1,0:T(8,128)}) custom-call(bf16[4,32,128]{2,1,0:T(8,128)(2,1)} %pad.4.pat_ref, s32[1,72]{1,0:T(1,128)} %bitcast.9, bf16[1,1024]{1,0:T(2,128)(2,1)} %reshape.19.query_ref, bf16[128,1024]{1,0:T(8,128)(2,1)} %kw_ref.1, bf16[128,1024]{1,0:T(8,128)(2,1)} %vw_ref.1, bf16[128,1024]{1,0:T(8,128)(2,1)} %ow_ref.1, ...), custom_call_target="tpu_custom_call" | custom-call | tf_op jit(solution)/shard_map/pallas_call | solution.py:432
  80.0 0.0 copy-start.1
  80.1 1.5 %copy.21 = bf16[32,1024]{1,0:T(8,128)(2,1)} copy(bf16[32,1024]{1,0:T(8,128)(2,1)} %get-tuple-element.4) | data formatting | bytes 131072
  81.5 0.0 copy-done.1
  81.5 0.6 copy.22
  (2 shorter events, 0.0 us)
Async XLA Ops:
  0.6 2.9 %copy-start = (bf16[48,4,1024]{2,1,0:T(4,128)(2,1)S(1)}, bf16[48,4,1024]{2,1,0:T(4,128)(2,1)}, u32[]{:S(2)}) copy-start(bf16[48,4,1024]{2,1,0:T(4,128)(2,1)} %param.11) | copy-start | bytes 1179652
  80.0 1.5 %copy-start.1 = (f32[18,512]{1,0:T(8,128)S(1)}, f32[18,512]{1,0:T(8,128)}, u32[]{:S(2)}) copy-start(f32[18,512]{1,0:T(8,128)} %get-tuple-element.5) | copy-start | bytes 110596

commit v4 on v3

--- a/solution.py
+++ b/solution.py
@@ -246,22 +246,23 @@
     pass_second((toks - lag) * (n_tok - 1) // toks + 1, n_tok)
 
     group = 4
-
-    @pl.loop(0, toks // group)
+    many = 8
+
+    @pl.loop(0, toks // many)
     def _(step):
-        first = step * group
-        flat = e_ref[pl.ds(first, group)].reshape(group * vars_, width)
+        first = step * many
+        flat = e_ref[pl.ds(first, many)].reshape(many * vars_, width)
         both = lax.dot_general(flat, wqb_ref[...], NT, preferred_element_type=F32)
-        both = both.reshape(group, vars_, 2 * H)
+        both = both.reshape(many, vars_, 2 * H)
         raw = (both[:, :, :H] + both[:, :, H:]) * (1.0 / math.sqrt(HD))
         squashed = jnp.tanh(raw * (1.0 / score_cap))
         exp_scores = jnp.exp(score_cap * squashed)
         attn = exp_scores / jnp.sum(exp_scores, axis=1, keepdims=True)
-        attn_ref[pl.ds(first, group)] = attn
-        slope_s_ref[pl.ds(first, group)] = (
+        attn_ref[pl.ds(first, many)] = attn
+        slope_s_ref[pl.ds(first, many)] = (
             attn * (1.0 - squashed * squashed) * (1.0 / math.sqrt(HD))
         )
-        for u in range(group):
+        for u in range(many):
             mixed = lax.dot_general(
                 attn[u].astype(BF), e_ref[first + u], TN, preferred_element_type=F32
             )
@@ -290,10 +291,10 @@
         cells = [g_ref[pl.ds(c * tall + t, H, stride=toks), :] for c in range(first, first + count)]
         return jnp.concatenate(cells, axis=1).astype(BF)
 
-    @pl.loop(0, toks // group)
+    @pl.loop(0, toks // many)
     def _(step):
-        for u in range(group):
-            t = step * group + u
+        for u in range(many):
+            t = step * many + u
             grad_attn = lax.dot_general(
                 e_ref[t], token_rows(t, 0, spans), NT, preferred_element_type=F32
             )

time: 82.4 us -> 81.5 us (0.989)
  Pallas kernels: 75.4 us -> 74.5 us
    pallas_call x1, Pallas kernels: 75.4 us -> 74.5 us  [compute(): pl.pallas_call(functools.partial(all_kernel, n_tok, n_var), out_shape=(ja...]
where the time goes in v4:
time: 81.5 us; the launch traced here: 81.2 us
  Pallas kernels  74.5 us (91%)
  local copies, waits for them, and re-layouts  5.01 us (6%)
  other arithmetic  1.02 us (1%)
    pallas_call x1, Pallas kernels, compute(): pl.pallas_call(functools.partial(all_kernel, n_tok, n_var), out_shape=(ja...  74.5 us
    unnamed x6, local copies, waits for them, and re-layouts  2.11 us

profile of v4, /device:TPU:27, one launch (start us, length us, event | category | flops | bytes accessed | tf_op | source)
XLA Modules:
  0.0 81.2 jit_solution(15925383881562913623)
XLA Ops:
  0.6 0.0 copy-start
  0.6 1.3 %reshape.19.query_ref = bf16[1,1024]{1,0:T(2,128)(2,1)} reshape(bf16[1024]{0:T(1024)(128)(2,1)} %param.13) | data formatting | bytes 4096 | tf_op jit(solution)/shard_map/reshape | solution.py:502
  2.0 0.8 reshape.16
  2.8 0.1 reshape.17
  2.9 0.6 pad.4.pat_ref
  3.6 0.0 copy-done
  3.6 1.0 %convert_bitcast_fusion.pw_ref = f32[4,48,1024]{2,1,0:T(8,128)} fusion(bf16[48,4,1024]{2,1,0:T(4,128)(2,1)S(1)} %copy-done), kind=kLoop, calls=%fused_computation | loop fusion | flops 196608 | bytes 1179648 | tf_op jit(solution)/shard_map/convert_element_type | solution.py:506
  4.6 74.5 %shard_map.104 = (bf16[32,1024]{1,0:T(8,128)(2,1)}, f32[18,512]{1,0:T(8,128)}) custom-call(bf16[4,32,128]{2,1,0:T(8,128)(2,1)} %pad.4.pat_ref, s32[1,72]{1,0:T(1,128)} %bitcast.9, bf16[1,1024]{1,0:T(2,128)(2,1)} %reshape.19.query_ref, bf16[128,1024]{1,0:T(8,128)(2,1)} %kw_ref.1, bf16[128,1024]{1,0:T(8,128)(2,1)} %vw_ref.1, bf16[128,1024]{1,0:T(8,128)(2,1)} %ow_ref.1, ...), custom_call_target="tpu_custom_call" | custom-call | tf_op jit(solution)/shard_map/pallas_call | solution.py:433
  79.1 0.0 copy-start.1
  79.1 1.5 %copy.21 = bf16[32,1024]{1,0:T(8,128)(2,1)} copy(bf16[32,1024]{1,0:T(8,128)(2,1)} %get-tuple-element.4) | data formatting | bytes 131072
  80.6 0.0 copy-done.1
  80.6 0.6 copy.22
  (2 shorter events, 0.0 us)
Async XLA Ops:
  0.6 2.9 %copy-start = (bf16[48,4,1024]{2,1,0:T(4,128)(2,1)S(1)}, bf16[48,4,1024]{2,1,0:T(4,128)(2,1)}, u32[]{:S(2)}) copy-start(bf16[48,4,1024]{2,1,0:T(4,128)(2,1)} %param.11) | copy-start | bytes 1179652
  79.1 1.5 %copy-start.1 = (f32[18,512]{1,0:T(8,128)S(1)}, f32[18,512]{1,0:T(8,128)}, u32[]{:S(2)}) copy-start(f32[18,512]{1,0:T(8,128)} %get-tuple-element.5) | copy-start | bytes 110596
